TPU v7x, 32 devices: a whole 2x2x4 slice. The times are simulated.
32 devices in a mesh: seq: 8 (over y, x, core), clip: 4 (over z).
Axes of the slice: x: 2, y: 2, z: 4, core: 2. Of those that a mesh axis runs over, the one named last changes fastest.
Arguments:
- frames_in: bfloat16 [4, 8, 128, 768], P('clip', 'seq'), may hold values from -6 to 6
- norm_gains: float32 [2, 768], replicated, may hold values from 0.5 to 1.5
- space_proj: bfloat16 [768, 2304], replicated, may hold values from -0.21875 to 0.21875
- space_out: bfloat16 [768, 768], replicated, may hold values from -0.21875 to 0.21875
- time_proj: bfloat16 [768, 2304], replicated, may hold values from -0.21875 to 0.21875
- time_out: bfloat16 [768, 768], replicated, may hold values from -0.21875 to 0.21875
- qk_gains: float32 [4, 768], replicated, may hold values from 1 to 2.5
Outputs:
- block_out: bfloat16 [4, 8, 128, 768], P('clip', 'seq')
- clip_embed: float32 [4, 768], P('clip')
- similarity: float32 [4, 4], P('clip')
All inputs are finite; a program needn't handle non-finite values.
Results may differ from a plain program's by a relative error of at most 0.02.
Values may be sent and summed in bfloat16 or wider, within the bound.
A program may use at most 64 MiB of HBM per device.

v0:
```python
import math

import jax
import jax.numpy as jnp
from jax import lax
from jax.sharding import PartitionSpec as P

D = 768
HEADS = 12


def layer_norm(values, gains_row):
    widened = values.astype(jnp.float32)
    average = jnp.mean(widened, axis=-1, keepdims=True)
    centred = widened - average
    spread = jnp.mean(centred * centred, axis=-1, keepdims=True)
    return (centred * lax.rsqrt(spread + 1e-05) * gains_row).astype(jnp.bfloat16)


def head_norm(values, gains_row):
    inverse = lax.rsqrt(jnp.mean(values * values, axis=-1, keepdims=True) + 1e-06)
    return (values * inverse * gains_row.reshape(HEADS, -1)).astype(jnp.bfloat16)


def project(normed, proj):
    channels = normed.shape[-1]
    leading = normed.shape[:-1]
    projected = jnp.dot(normed.reshape(-1, channels), proj, preferred_element_type=jnp.float32)
    return projected.astype(jnp.bfloat16).reshape(leading + (proj.shape[1],))


def attention(projected, out_weight, gain_query, gain_key):
    channels = out_weight.shape[0]
    leading = projected.shape[:-1]
    head_size = channels // HEADS
    queries = projected[..., :channels].astype(jnp.float32).reshape(leading + (HEADS, head_size))
    key_part = (
        projected[..., channels : 2 * channels]
        .astype(jnp.float32)
        .reshape(leading + (HEADS, head_size))
    )
    value_part = projected[..., 2 * channels :].reshape(leading + (HEADS, head_size))
    query_n = head_norm(queries, gain_query)
    key_n = head_norm(key_part, gain_key)
    scores = jnp.einsum("...lhe,...mhe->...hlm", query_n, key_n, preferred_element_type=jnp.float32)
    scores = scores * (1.0 / math.sqrt(head_size))
    raised = jnp.exp(scores)
    attn_weights = (raised / jnp.sum(raised, axis=-1, keepdims=True)).astype(jnp.bfloat16)
    context = jnp.einsum(
        "...hlm,...mhe->...lhe", attn_weights, value_part, preferred_element_type=jnp.float32
    )
    context = context.astype(jnp.bfloat16).reshape(-1, channels)
    branch = jnp.dot(context, out_weight, preferred_element_type=jnp.float32)
    return branch.reshape(leading + (channels,))


def on_device(frames_in, norm_gains, space_proj, space_out, time_proj, time_out, qk_gains):
    clips_here, frames_here, patch_count, channels = frames_in.shape
    groups = lax.axis_size("seq")
    per_group = patch_count // groups
    spatial_in = layer_norm(frames_in, norm_gains[0])
    branch = attention(project(spatial_in, space_proj), space_out, qk_gains[0], qk_gains[1])
    middle = (frames_in.astype(jnp.float32) + branch).astype(jnp.bfloat16)
    temporal_in = layer_norm(middle, norm_gains[1])
    outgoing = temporal_in.reshape(clips_here, groups, per_group, frames_here, channels)
    arrived = attention(
        project(
            lax.all_to_all(outgoing, "seq", split_axis=1, concat_axis=3, tiled=True), time_proj
        ),
        time_out,
        qk_gains[2],
        qk_gains[3],
    ).astype(jnp.bfloat16)
    returned = lax.all_to_all(arrived, "seq", split_axis=3, concat_axis=1, tiled=True)
    returned = returned.reshape(clips_here, frames_here, patch_count, channels)
    block_out = (middle.astype(jnp.float32) + returned.astype(jnp.float32)).astype(jnp.bfloat16)
    local_sum = jnp.sum(block_out.astype(jnp.float32), axis=(1, 2))
    pooled_total = lax.psum(local_sum, "seq")
    pooled = pooled_total / (frames_here * patch_count * groups)
    clip_embed = pooled * lax.rsqrt(jnp.mean(pooled * pooled, axis=-1, keepdims=True) + 1e-06)
    all_embeds = lax.all_gather(clip_embed, "clip", axis=0, tiled=True)
    similarity = (
        jnp.dot(
            clip_embed,
            all_embeds.T,
            precision=lax.Precision.HIGHEST,
            preferred_element_type=jnp.float32,
        )
        / D
    )
    return (block_out, clip_embed, similarity)


def solution(mesh):
    return jax.shard_map(
        on_device,
        mesh=mesh,
        in_specs=(P("clip", "seq", None, None), P(), P(), P(), P(), P(), P()),
        out_specs=(P("clip", "seq", None, None), P("clip", None), P("clip", None)),
        check_vma=False,
    )
```

profile of v0, /device:TPU:0, one launch (start us, length us, event | category | flops | bytes accessed | tf_op | source)
XLA Modules:
  0.0 115.0 jit_solution(2321447138677148695)
XLA Ops:
  0.6 1.5 %slice_reduce_fusion.2 = (f32[768]{0:T(1024)}, f32[768]{0:T(1024)S(1)}) fusion(f32[2,768]{1,0:T(2,128)} %param.8), kind=kLoop, calls=%fused_computation.74 | loop fusion | bytes 12288 | tf_op jit(solution)/shard_map/slice | solution.py:64
  2.1 1.0 convert_reduce_fusion
  3.2 1.1 fusion.20
  4.3 1.6 %fusion = bf16[1,1,128,2304]{3,2,1,0:T(8,128)(2,1)S(1)} fusion(bf16[768,2304]{1,0:T(8,128)(2,1)S(1)} %copy-done, bf16[1,1,128,768]{3,2,1,0:T(8,128)(2,1)} %param.7, f32[768]{0:T(1024)S(1)} %get-tuple-element.8, f32[128]{0:T(128)S(1)} %add_rsqrt_fusion.5, f32[128]{0:T(128)S(1)} %broadcast_multiply_fusion.2), kind=kOutput, calls=%fused_computation.2 | convolution fusion | flops 453771264 | bytes 4329472 | tf_op jit(solution)/shard_map/dot_general | solution.py:28
  5.9 0.9 fusion.41
  6.9 1.0 slice_convert_fusion.2
  7.8 1.9 %copy.31 = f32[1,1,128,768]{2,3,1,0:T(8,128)} copy(f32[1,1,128,768]{3,2,1,0:T(8,128)} %get-tuple-element.16) | data formatting | bytes 786432 | tf_op jit(solution)/shard_map/mul | solution.py:21
  9.7 1.9 %copy.33 = f32[1,1,128,768]{2,3,1,0:T(8,128)} copy(f32[1,1,128,768]{3,2,1,0:T(8,128)} %get-tuple-element.17) | data formatting | bytes 786432 | tf_op jit(solution)/shard_map/mul | solution.py:21
  11.7 1.6 %reduce_sum.112 = f32[128,12]{0,1:T(8,128)} reduce(f32[128,12,64]{0,2,1:T(8,128)} %bitcast.92, f32[]{:T(128)} %constant.28.clone.1), dimensions={2}, to_apply=%region_2.0 | reduce | flops 96768 | bytes 399364 | tf_op jit(solution)/shard_map/reduce_sum | solution.py:21
  13.3 1.6 %reduce_sum.113 = f32[128,12]{0,1:T(8,128)} reduce(f32[128,12,64]{0,2,1:T(8,128)} %bitcast.93, f32[]{:T(128)} %constant.28.clone.1), dimensions={2}, to_apply=%region_3.0 | reduce | flops 96768 | bytes 399364 | tf_op jit(solution)/shard_map/reduce_sum | solution.py:21
  14.9 1.9 %copy.30 = f32[1,1,128,768]{2,3,1,0:T(8,128)} copy(f32[1,1,128,768]{3,2,1,0:T(8,128)} %get-tuple-element.19) | data formatting | bytes 786432 | tf_op jit(solution)/shard_map/convert_element_type | solution.py:36
  16.8 1.9 %copy.32 = f32[1,1,128,768]{2,3,1,0:T(8,128)} copy(f32[1,1,128,768]{3,2,1,0:T(8,128)} %get-tuple-element.18) | data formatting | bytes 786432 | tf_op jit(solution)/shard_map/convert_element_type | solution.py:39
  18.7 1.5 %slice_reduce_fusion.1 = (f32[768]{0:T(1024)}, f32[768]{0:T(1024)}, f32[768]{0:T(1024)S(1)}, f32[768]{0:T(1024)}) fusion(f32[4,768]{1,0:T(4,128)} %param.13), kind=kLoop, calls=%fused_computation.73 | loop fusion | bytes 24576 | tf_op jit(solution)/shard_map/slice | solution.py:71
  20.3 0.8 mul.250
  21.1 1.7 %copy.29 = bf16[1,1,128,768]{2,3,1,0:T(8,128)(2,1)} copy(bf16[1,1,128,768]{3,2,1,0:T(8,128)(2,1)} %get-tuple-element.20) | data formatting | bytes 393216 | tf_op jit(solution)/shard_map/slice | solution.py:42
  22.8 0.7 add_rsqrt_fusion.2
  23.5 2.6 %fusion.3 = f32[12,128,128]{1,2,0:T(8,128)} fusion(f32[128,12,64]{0,2,1:T(8,128)} %bitcast.94, f32[128,12,64]{0,2,1:T(8,128)} %bitcast.95, f32[12,64]{1,0:T(8,128)S(1)} %mul.250, f32[128,12]{0,1:T(8,128)S(1)} %get-tuple-element.23, f32[12,64]{1,0:T(8,128)S(1)} %mul.243, f32[128,12]{0,1:T(8,128)S(1)} %get-tuple-element.24), kind=kOutput, calls=%fused_computation.7 | convolution fusion | flops 25952256 | bytes 1591296 | tf_op jit(solution)/shard_map/...lhe,...mhe->...hlm/dot_general | solution.py:45
  26.1 2.4 %convolution_convert_fusion.3 = bf16[12,64,128]{2,1,0:T(8,128)(2,1)} fusion(bf16[128,12,64]{0,2,1:T(8,128)(2,1)} %bitcast.98, f32[12,128,128]{1,2,0:T(8,128)} %fusion.3), kind=kOutput, calls=%fused_computation.17 | convolution fusion | flops 25659008 | bytes 1179648 | tf_op jit(solution)/shard_map/...hlm,...mhe->...lhe/dot_general | solution.py:49
  28.5 1.8 %fusion.58 = (f32[128]{0:T(128)S(1)}, f32[1,1,128,768]{3,2,1,0:T(8,128)S(1)}) fusion(bf16[128,768]{0,1:T(8,128)(2,1)} %bitcast.97, bf16[768,768]{1,0:T(8,128)(2,1)} %param.10, bf16[1,1,128,768]{3,2,1,0:T(8,128)(2,1)} %param.7), kind=kOutput, calls=%fused_computation.88 | convolution fusion | flops 151486336 | bytes 1966592 | tf_op jit(solution)/shard_map/dot_general | solution.py:53
  30.5 0.5 copy-done.1
  31.1 0.8 multiply_convert_fusion.2
  31.9 5.2 %all-to-all-start = ((bf16[1,8,16,1,768]{4,2,3,0,1:T(8,128)(2,1)}), bf16[1,8,16,1,768]{4,2,3,0,1:T(8,128)(2,1)}, u32[]{:S(2)}, u32[]{:S(2)}) async-start(bf16[1,8,16,1,768]{4,2,3,0,1:T(8,128)(2,1)} %bitcast.96), calls=%async_computation | async-start | bytes 393216 | tf_op jit(solution)/shard_map/all_to_all | solution.py:68
  37.1 0.8 mul.272
  37.9 5.5 %all-to-all-done = bf16[1,8,16,1,768]{4,2,3,0,1:T(8,128)(2,1)} async-done(((bf16[1,8,16,1,768]{4,2,3,0,1:T(8,128)(2,1)}), bf16[1,8,16,1,768]{4,2,3,0,1:T(8,128)(2,1)}, u32[]{:S(2)}, u32[]{:S(2)}) %all-to-all-start) | async-done | bytes 196640 | tf_op jit(solution)/shard_map/all_to_all | solution.py:68
  43.4 2.8 %fusion.1 = bf16[1,1,16,8,2304]{4,3,2,1,0:T(8,128)(2,1)S(1)} fusion(bf16[768,2304]{1,0:T(8,128)(2,1)} %param.11, bf16[1,8,16,1,768]{4,2,3,0,1:T(8,128)(2,1)} %all-to-all-done), kind=kOutput, calls=%fused_computation.3 | convolution fusion | flops 453279744 | bytes 4325376 | tf_op jit(solution)/shard_map/dot_general | solution.py:28
  46.2 1.0 fusion.57
  47.1 1.0 fusion.43
  48.1 2.2 %reshape.331 = f32[16,8,12,64]{3,2,1,0:T(8,128)} reshape(f32[1,1,16,8,768]{4,3,2,1,0:T(8,128)} %get-tuple-element.13) | data formatting | bytes 786432 | tf_op jit(solution)/shard_map/reshape | solution.py:36
  50.3 2.3 %mul.262 = f32[16,8,12,64]{3,2,1,0:T(8,128)} reshape(f32[1,1,16,8,768]{4,3,2,1,0:T(8,128)} %get-tuple-element.14) | data formatting | bytes 786432 | tf_op jit(solution)/shard_map/mul | solution.py:21
  52.6 2.2 %reduce_sum.117 = f32[16,8,12]{2,1,0:T(8,128)} reduce(f32[16,8,12,64]{3,2,1,0:T(8,128)} %mul.262, f32[]{:T(128)} %constant.28.clone.1), dimensions={3}, to_apply=%region_7.0 | reduce | flops 96768 | bytes 399364 | tf_op jit(solution)/shard_map/reduce_sum | solution.py:21
  54.8 1.5 %add_rsqrt_fusion.1 = f32[16,8,12]{2,1,0:T(8,128)} fusion(f32[16,8,12]{2,1,0:T(8,128)} %reduce_sum.117), kind=kLoop, calls=%fused_computation.65 | loop fusion | flops 3072 | bytes 12288 | tf_op jit(solution)/shard_map/rsqrt | solution.py:21
  56.3 2.3 %reshape.332 = f32[16,8,12,64]{3,2,1,0:T(8,128)} reshape(f32[1,1,16,8,768]{4,3,2,1,0:T(8,128)} %get-tuple-element.12) | data formatting | bytes 786432 | tf_op jit(solution)/shard_map/reshape | solution.py:40
  58.5 2.2 %mul.269 = f32[16,8,12,64]{3,2,1,0:T(8,128)} reshape(f32[1,1,16,8,768]{4,3,2,1,0:T(8,128)} %get-tuple-element.15) | data formatting | bytes 786432 | tf_op jit(solution)/shard_map/mul | solution.py:21
  60.8 2.2 %reduce_sum.118 = f32[16,8,12]{2,1,0:T(8,128)} reduce(f32[16,8,12,64]{3,2,1,0:T(8,128)} %mul.269, f32[]{:T(128)} %constant.28.clone.1), dimensions={3}, to_apply=%region_8.0 | reduce | flops 96768 | bytes 399364 | tf_op jit(solution)/shard_map/reduce_sum | solution.py:21
  63.0 1.5 %add_rsqrt_fusion = f32[16,8,12]{2,1,0:T(8,128)} fusion(f32[16,8,12]{2,1,0:T(8,128)} %reduce_sum.118), kind=kLoop, calls=%fused_computation.64 | loop fusion | flops 3072 | bytes 12288 | tf_op jit(solution)/shard_map/rsqrt | solution.py:21
  64.4 2.1 %reshape.330 = bf16[16,8,12,64]{3,2,1,0:T(8,128)(2,1)} reshape(bf16[1,1,16,8,768]{4,3,2,1,0:T(8,128)(2,1)} %get-tuple-element.11) | data formatting | bytes 393216 | tf_op jit(solution)/shard_map/reshape.45
  66.5 1.7 %multiply_convert_fusion.1 = bf16[16,8,12,64]{3,2,1,0:T(8,128)(2,1)S(1)} fusion(f32[16,8,12,64]{3,2,1,0:T(8,128)} %reshape.331, f32[12,64]{1,0:T(8,128)S(1)} %mul.265, f32[16,8,12]{2,1,0:T(8,128)} %add_rsqrt_fusion.1), kind=kLoop, calls=%fused_computation.23 | loop fusion | flops 294912 | bytes 599040 | tf_op jit(solution)/shard_map/convert_element_type | solution.py:22
  68.5 1.2 %fusion.2 = f32[16,12,8,8]{2,3,1,0:T(8,128)} fusion(bf16[16,8,12,64]{3,2,1,0:T(8,128)(2,1)S(1)} %multiply_convert_fusion, bf16[16,8,12,64]{3,2,1,0:T(8,128)(2,1)S(1)} %multiply_convert_fusion.1), kind=kOutput, calls=%fused_computation.5 | convolution fusion | flops 1585152 | bytes 442368 | tf_op jit(solution)/shard_map/...lhe,...mhe->...hlm/dot_general | solution.py:45
  69.8 2.8 %fusion.4 = bf16[1,1,16,8,12,64]{5,3,4,2,1,0:T(8,128)(2,1)} fusion(f32[16,12,8,8]{2,3,1,0:T(8,128)} %fusion.2, bf16[16,8,12,64]{3,2,1,0:T(8,128)(2,1)} %reshape.330), kind=kOutput, calls=%fused_computation.9 | convolution fusion | flops 1697287 | bytes 442368 | tf_op jit(solution)/shard_map/...hlm,...mhe->...lhe/dot_general | solution.py:49
  72.5 1.9 %copy.41 = bf16[1,1,16,8,12,64]{5,4,3,2,1,0:T(8,128)(2,1)} copy(bf16[1,1,16,8,12,64]{5,3,4,2,1,0:T(8,128)(2,1)} %fusion.4) | data formatting | bytes 393216 | tf_op jit(solution)/shard_map/convert_element_type | solution.py:52
  74.4 2.1 %dot_general.36 = bf16[16,8,768]{2,1,0:T(8,128)(2,1)} reshape(bf16[1,1,16,8,12,64]{5,4,3,2,1,0:T(8,128)(2,1)} %copy.41) | data formatting | bytes 393216 | tf_op jit(solution)/shard_map/dot_general | solution.py:53
  76.5 1.7 %fusion.13 = bf16[1,1,16,8,768]{4,3,2,1,0:T(8,128)(2,1)S(1)} fusion(bf16[16,8,768]{2,1,0:T(8,128)(2,1)} %dot_general.36, bf16[768,768]{1,0:T(8,128)(2,1)} %param.12), kind=kOutput, calls=%fused_computation.18 | convolution fusion | flops 151093248 | bytes 1572864 | tf_op jit(solution)/shard_map/dot_general | solution.py:53
  78.3 8.6 %all_to_all.24 = bf16[1,1,16,8,768]{4,2,1,0,3:T(8,128)(2,1)S(1)} all-to-all(bf16[1,1,16,8,768]{4,2,1,0,3:T(8,128)(2,1)S(1)} %copy.42), channel_id=1, replica_groups=mesh['seq'=8,'clip'=4] {'seq'}, dimensions={3} | all-to-all | bytes 393216 | tf_op jit(solution)/shard_map/all_to_all | solution.py:74
  87.0 0.7 convert_reduce_fusion.1
  87.7 11.8 %psum.7 = f32[1,768]{1,0:T(1,128)S(1)} all-reduce(f32[1,768]{1,0:T(1,128)S(1)} %reduce_sum.121), channel_id=1, replica_groups=mesh['seq'=8,'clip'=4] {'seq'}, use_global_device_ids=true, to_apply=%region_11.0 | all-reduce | flops 768 | bytes 6144 | tf_op jit(solution)/shard_map/psum | solution.py:78
  99.5 0.6 multiply_reduce_fusion.1
  100.8 13.5 %all-gather = f32[4,1,768]{2,1,0:T(1,128)S(1)} all-gather(f32[1,1,768]{2,1,0:T(1,128)S(1)} %fusion.67), channel_id=1, replica_groups=mesh['seq'=8,'clip'=4] {'clip'}, dimensions={0}, use_global_device_ids=true | all-gather | bytes 15360 | tf_op jit(solution)/shard_map/all_gather | solution.py:81
  114.3 0.7 fusion.17
  (28 shorter events, 0.8 us)
Async XLA Ops:
  0.6 3.7 %copy-start = (bf16[768,2304]{1,0:T(8,128)(2,1)S(1)}, bf16[768,2304]{1,0:T(8,128)(2,1)}, u32[]{:S(2)}) copy-start(bf16[768,2304]{1,0:T(8,128)(2,1)} %param.9) | copy-start | bytes 10616836
  28.5 2.5 %copy-start.5 = (f32[768]{0:T(1024)S(1)}, f32[768]{0:T(1024)}, u32[]{:S(2)}) copy-start(f32[768]{0:T(1024)} %get-tuple-element.7) | copy-start | bytes 9220
  30.3 0.8 copy-start.1
  30.3 6.7 %copy-start.6 = (f32[768]{0:T(1024)S(1)}, f32[768]{0:T(1024)}, u32[]{:S(2)}) copy-start(f32[768]{0:T(1024)} %get-tuple-element.3) | copy-start | bytes 9220
  31.9 11.5 %all-to-all-start = ((bf16[1,8,16,1,768]{4,2,3,0,1:T(8,128)(2,1)}), bf16[1,8,16,1,768]{4,2,3,0,1:T(8,128)(2,1)}, u32[]{:S(2)}, u32[]{:S(2)}) async-start(bf16[1,8,16,1,768]{4,2,3,0,1:T(8,128)(2,1)} %bitcast.96), calls=%async_computation | async-start | bytes 393216 | tf_op jit(solution)/shard_map/all_to_all | solution.py:68
  66.5 1.7 %copy-start.3 = (f32[16,8,12,64]{3,2,1,0:T(8,128)S(1)}, f32[16,8,12,64]{3,2,1,0:T(8,128)}, u32[]{:S(2)}) copy-start(f32[16,8,12,64]{3,2,1,0:T(8,128)} %reshape.332) | copy-start | bytes 1179652
  66.5 1.7 %copy-start.4 = (f32[16,8,12]{2,1,0:T(8,128)S(1)}, f32[16,8,12]{2,1,0:T(8,128)}, u32[]{:S(2)}) copy-start(f32[16,8,12]{2,1,0:T(8,128)} %add_rsqrt_fusion) | copy-start | bytes 18436
  76.5 10.5 %copy-start.2 = (f32[1,1,128,768]{3,2,1,0:T(8,128)S(1)}, f32[1,1,128,768]{3,2,1,0:T(8,128)}, u32[]{:S(2)}) copy-start(f32[1,1,128,768]{3,2,1,0:T(8,128)} %copy-done.1) | copy-start | bytes 1179652
  100.8 14.2 %copy-start.7 = (f32[1,768]{1,0:T(1,128)}, f32[1,768]{1,0:T(1,128)S(1)}, u32[]{:S(2)}) copy-start(f32[1,768]{1,0:T(1,128)S(1)} %broadcast_multiply_fusion) | copy-start | bytes 9220
where the time goes:
time: 116 us; the launch traced here: 115 us
  blocking collectives  33.9 us (29%)
  local copies, waits for them, and re-layouts  29.6 us (26%)
  other arithmetic  21.6 us (19%)
  matrix products  17.6 us (15%)
  waiting for transfers between devices  5.51 us (5%)
  starting transfers between devices  5.17 us (4%)
  between operations  1.51 us (1%)
    all_gather x1, blocking collectives, on_device(): all_embeds = lax.all_gather(clip_embed, 'clip', axis=0, tiled=True)  13.5 us
    psum x1, blocking collectives, on_device(): pooled_total = lax.psum(local_sum, 'seq')  11.8 us
    all_to_all x1, blocking collectives, on_device(): lax.all_to_all(arrived, 'seq', split_axis=3, concat_axis=1, tiled=True)  8.63 us
    mul x4, local copies, waits for them, and re-layouts, head_norm(): values * values  8.34 us
    reduce_sum x4, other arithmetic, head_norm(): jnp.mean(values * values, axis=-1, keepdims=True) + 1e-06  7.62 us
    all_to_all x1, waiting for transfers between devices, on_device(): lax.all_to_all(outgoing, 'seq', split_axis=1, concat_axis=3, tiled=True)  5.51 us
    all_to_all x1, starting transfers between devices, on_device(): lax.all_to_all(outgoing, 'seq', split_axis=1, concat_axis=3, tiled=True)  5.17 us
    dot_general x2, matrix products, attention(): jnp.einsum('...hlm,...mhe->...lhe', attn_weights, value_part, preferred_e...  5.16 us
  transfers between devices with their start and end apart: 1, of which 1 were waited for; matrix products, arithmetic and copies ran while one was open for 1% of the time, Pallas kernels for 0%

commit v1 on v0

v1 whole, which is shorter than its diff:
```python
import functools

import jax
import jax.numpy as jnp
from jax import lax
from jax.experimental import pallas as pl
from jax.experimental.pallas import tpu as pltpu
from jax.sharding import PartitionSpec as P

D = 768
HEADS = 12
HEAD = D // HEADS
WIDE = 4 * HEAD
MESH = pl.DeviceIdType.MESH
BF16 = jnp.bfloat16
F32 = jnp.float32


def each(count, body):
    if count <= 8:
        for at in range(1, count):
            body(at)
    else:
        lax.fori_loop(1, count, lambda at, carry: (body(at), carry)[1], 0)


def layer_norm(widened, gain):
    average = jnp.mean(widened, axis=-1, keepdims=True)
    centred = widened - average
    spread = jnp.mean(centred * centred, axis=-1, keepdims=True)
    return (centred * lax.rsqrt(spread + 1e-05) * gain).astype(BF16)


def attend(tokens, proj, out_weight, gains, query_row, mask, waits):
    row = lax.broadcasted_iota(jnp.int32, (WIDE, WIDE), 0) // HEAD
    col = lax.broadcasted_iota(jnp.int32, (WIDE, WIDE), 1) // HEAD
    averager = jnp.where(row == col, 1.0 / HEAD, 0.0).astype(BF16)
    count = tokens.shape[0]
    low = lax.broadcasted_iota(jnp.int32, (count, 2 * HEAD), 1) < HEAD
    zero = jnp.zeros((count, 2 * HEAD), BF16)
    ones = jnp.ones((count, 2 * HEAD), BF16)
    ones_low, ones_high = jnp.where(low, ones, zero), jnp.where(low, zero, ones)

    def part(at):
        return jnp.dot(tokens, proj[:, at : at + WIDE], preferred_element_type=F32).astype(BF16)

    def normed(at, gain):
        values = part(at).astype(F32)
        mean = jnp.dot((values * values).astype(BF16), averager, preferred_element_type=F32)
        return (values * lax.rsqrt(mean + 1e-06) * gain).astype(BF16)

    waits[0]()
    context = []
    for at in range(0, D, WIDE):
        queries = normed(at, gains[query_row : query_row + 1, at : at + WIDE] * (HEAD ** -0.5))
        keys = normed(D + at, gains[query_row + 1 : query_row + 2, at : at + WIDE])
        values = part(2 * D + at)
        for here in range(0, WIDE, 2 * HEAD):
            query = queries[:, here : here + 2 * HEAD]
            key = keys[:, here : here + 2 * HEAD]
            value = values[:, here : here + 2 * HEAD]
            key_pair = jnp.concatenate([jnp.where(low, key, zero), jnp.where(low, zero, key)], axis=0)
            scores = lax.dot_general(query, key_pair, (((1,), (1,)), ((), ())), preferred_element_type=F32)
            raised = jnp.exp(scores).astype(BF16)
            if mask is not None:
                raised = raised * mask
            value_pair = jnp.concatenate(
                [
                    jnp.concatenate([jnp.where(low, value, zero), ones_low], axis=1),
                    jnp.concatenate([jnp.where(low, zero, value), ones_high], axis=1),
                ],
                axis=0,
            )
            both = jnp.dot(raised, value_pair, preferred_element_type=F32)
            context.append((both[:, : 2 * HEAD] / both[:, 2 * HEAD :]).astype(BF16))
    waits[1]()
    return jnp.dot(jnp.concatenate(context, axis=1), out_weight[...], preferred_element_type=F32)


def kernel(
    groups, clips, per, tokens_in_clip,
    frames_ref, norm_ref, space_proj_hbm, space_out_hbm, time_proj_hbm, time_out_hbm, qk_ref,
    block_ref, embed_ref, similar_ref,
    space_proj, space_out, time_proj, time_out,
    outgoing, arrived, branch_out, returned, sums, embeds,
    weight_sem, out_send, out_recv, back_send, back_recv, sum_send, sum_recv, embed_send, embed_recv,
):
    me = lax.axis_index("seq")
    clip = lax.axis_index("clip")
    patches = frames_ref.shape[0]
    padded = outgoing.shape[1]

    loads = [
        pltpu.make_async_copy(source, target, weight_sem.at[at])
        for at, (source, target) in enumerate(
            [(space_proj_hbm, space_proj), (space_out_hbm, space_out), (time_proj_hbm, time_proj), (time_out_hbm, time_out)]
        )
    ]
    for load in loads:
        load.start()

    barrier = pltpu.get_barrier_semaphore()
    each(groups, lambda d: pl.semaphore_signal(
        barrier, inc=1, device_id={"seq": lax.rem(me + d, groups)}, device_id_type=MESH))
    each(clips, lambda d: pl.semaphore_signal(
        barrier, inc=1, device_id={"clip": lax.rem(clip + d, clips)}, device_id_type=MESH))

    def to_group(source, target, send, recv, peer):
        return pltpu.make_async_remote_copy(
            src_ref=source, dst_ref=target, send_sem=send, recv_sem=recv,
            device_id={"seq": peer}, device_id_type=MESH)

    def outward(d):
        peer = lax.rem(me + d, groups)
        return to_group(outgoing.at[peer], arrived.at[d], out_send.at[d], out_recv.at[d], peer)

    def homeward(d):
        peer = lax.rem(me + (groups - d), groups)
        return to_group(branch_out.at[d], returned.at[me], back_send.at[d], back_recv.at[d], peer)

    def share(d):
        return to_group(sums.at[0], sums.at[d], sum_send.at[d], sum_recv.at[d], lax.rem(me + d, groups))

    def announce(d):
        return pltpu.make_async_remote_copy(
            src_ref=embeds.at[clip], dst_ref=embeds.at[clip], send_sem=embed_send.at[d], recv_sem=embed_recv.at[d],
            device_id={"clip": lax.rem(clip + d, clips)}, device_id_type=MESH)

    frames = frames_ref[...].astype(F32)
    spread_out = attend(
        layer_norm(frames, norm_ref[0:1, :]), space_proj, space_out, qk_ref, 0, None,
        (loads[0].wait, loads[1].wait))
    middle = (frames + spread_out).astype(BF16)
    widened = middle.astype(F32)
    ready = layer_norm(widened, norm_ref[1:2, :])
    if padded != per:
        place = lax.broadcasted_iota(jnp.int32, (groups * padded, patches), 0)
        token = lax.broadcasted_iota(jnp.int32, (groups * padded, patches), 1)
        chosen = (token == place // padded * per + place % padded) & (place % padded < per)
        spread = jnp.where(chosen, 1.0, 0.0).astype(BF16)
        ready = jnp.dot(spread, ready, preferred_element_type=F32).astype(BF16)
    outgoing[...] = ready.reshape(outgoing.shape)
    pl.semaphore_wait(barrier, groups - 1 + clips - 1)
    each(groups, lambda d: outward(d).start())
    arrived[0] = outgoing[me]
    own_sum = jnp.sum(widened, axis=0, keepdims=True)

    row = lax.broadcasted_iota(jnp.int32, (groups * per, groups * per), 0) % per
    col = lax.broadcasted_iota(jnp.int32, (groups * per, groups * per), 1) % per
    same = jnp.where(row == col, 1.0, 0.0).astype(BF16)
    each(groups, lambda d: outward(d).wait_recv())
    tokens = arrived[...].reshape(groups * padded, D)
    if padded != per:
        gather = jnp.where(chosen.T, 1.0, 0.0).astype(BF16)
        tokens = jnp.dot(gather, tokens, preferred_element_type=F32).astype(BF16)
    branch = attend(
        tokens, time_proj, time_out, qk_ref, 2, jnp.concatenate([same, same], axis=1),
        (loads[2].wait, loads[3].wait)).astype(BF16)
    sums[0] = own_sum + jnp.sum(branch.astype(F32), axis=0, keepdims=True)
    each(groups, lambda d: share(d).start())
    if padded != per:
        branch = jnp.dot(spread, branch, preferred_element_type=F32).astype(BF16)
    branch_out[...] = branch.reshape(branch_out.shape)
    each(groups, lambda d: homeward(d).start())
    returned[me] = branch_out[0]

    each(groups, lambda d: share(d).wait_recv())
    pooled = jnp.sum(sums[...], axis=0) / tokens_in_clip
    embed = pooled * lax.rsqrt(jnp.mean(pooled * pooled, axis=-1, keepdims=True) + 1e-06)
    embeds[clip] = embed
    each(clips, lambda d: announce(d).start())
    embed_ref[...] = embed

    each(groups, lambda d: homeward(d).wait_recv())
    back = returned[...].reshape(groups * padded, D)
    if padded != per:
        back = jnp.dot(gather, back, preferred_element_type=F32).astype(BF16)
    block_ref[...] = (widened + back.astype(F32)).astype(BF16)

    each(clips, lambda d: announce(d).wait_recv())
    products = jnp.sum(embeds[...] * embed[None], axis=-1, keepdims=True)[:, 0, :] / D
    row = lax.broadcasted_iota(jnp.int32, (clips, clips), 0)
    col = lax.broadcasted_iota(jnp.int32, (clips, clips), 1)
    similar_ref[...] = jnp.sum(jnp.where(row == col, products, 0.0), axis=0, keepdims=True)

    each(groups, lambda d: outward(d).wait_send())
    each(groups, lambda d: share(d).wait_send())
    each(groups, lambda d: homeward(d).wait_send())
    each(clips, lambda d: announce(d).wait_send())


def on_device(frames_in, norm_gains, space_proj, space_out, time_proj, time_out, qk_gains):
    groups, clips = lax.axis_size("seq"), lax.axis_size("clip")
    _, _, patches, channels = frames_in.shape
    per = patches // groups
    padded = -(-per // 16) * 16
    vmem = pl.BlockSpec(memory_space=pltpu.VMEM)
    hbm = pl.BlockSpec(memory_space=pl.ANY)
    blocks = pltpu.VMEM((groups, padded, channels), BF16)
    dma = pltpu.SemaphoreType.DMA
    block, embed, similar = pl.pallas_call(
        functools.partial(kernel, groups, clips, per, patches * groups),
        out_shape=(
            jax.ShapeDtypeStruct((patches, channels), BF16),
            jax.ShapeDtypeStruct((1, channels), F32),
            jax.ShapeDtypeStruct((1, clips), F32),
        ),
        in_specs=[vmem, vmem, hbm, hbm, hbm, hbm, vmem],
        out_specs=(vmem, vmem, vmem),
        scratch_shapes=[
            pltpu.VMEM(space_proj.shape, BF16),
            pltpu.VMEM(space_out.shape, BF16),
            pltpu.VMEM(time_proj.shape, BF16),
            pltpu.VMEM(time_out.shape, BF16),
            blocks, blocks, blocks, blocks,
            pltpu.VMEM((groups, 1, channels), F32),
            pltpu.VMEM((clips, 1, channels), F32),
            dma((4,)),
            dma((groups,)), dma((groups,)), dma((groups,)), dma((groups,)),
            dma((groups,)), dma((groups,)), dma((clips,)), dma((clips,)),
        ],
        compiler_params=pltpu.CompilerParams(
            collective_id=0, has_side_effects=True, vmem_limit_bytes=48 * 1024 * 1024),
    )(frames_in.reshape(patches, channels), norm_gains, space_proj, space_out, time_proj, time_out, qk_gains)
    return block.reshape(frames_in.shape), embed, similar


def solution(mesh):
    return jax.shard_map(
        on_device,
        mesh=mesh,
        in_specs=(P("clip", "seq", None, None), P(), P(), P(), P(), P(), P()),
        out_specs=(P("clip", "seq", None, None), P("clip", None), P("clip", None)),
        check_vma=False,
    )
```

time: 116 us -> 29.9 us (0.26)
  blocking collectives: 33.9 us -> 0 us
  local copies, waits for them, and re-layouts: 29.6 us -> 6.62 us
  Pallas kernels: 0 us -> 22.4 us
  other arithmetic: 21.6 us -> 0 us
  matrix products: 17.6 us -> 0 us
  waiting for transfers between devices: 5.51 us -> 0 us
  starting transfers between devices: 5.17 us -> 0 us
    pallas_call x0 -> x1, Pallas kernels: none -> 22.4 us  [on_device(): pl.pallas_call(functools.partial(kernel, groups, clips, per, patches * gr...]
    dot_general x9 -> x0, matrix products: 17.6 us -> none  [the longest x2 5.16 us: attention(): jnp.einsum('...hlm,...mhe->...lhe', attn_weights, value_part, preferred_e...]
    all_gather x1 -> x0, blocking collectives: 13.5 us -> none  [on_device(): all_embeds = lax.all_gather(clip_embed, 'clip', axis=0, tiled=True)]
    psum x1 -> x0, blocking collectives: 11.8 us -> none  [on_device(): pooled_total = lax.psum(local_sum, 'seq')]
    reduce_sum x9 -> x0, other arithmetic: 11.3 us -> none  [the longest x4 7.62 us: head_norm(): jnp.mean(values * values, axis=-1, keepdims=True) + 1e-06]
    mul x8 -> x0, local copies, waits for them, and re-layouts: 9.98 us -> none  [the longest x4 8.34 us: head_norm(): values * values]
    all_to_all x1 -> x0, blocking collectives: 8.63 us -> none  [on_device(): lax.all_to_all(arrived, 'seq', split_axis=3, concat_axis=1, tiled=True)]
    unnamed x16 -> x13, local copies, waits for them, and re-layouts: 0.56 us -> 6.62 us
  transfers between devices with their start and end apart: 1 -> 0, of which waited for: 1 -> 0; matrix products, arithmetic and copies ran while one was open for 1% -> 0% of each run, Pallas kernels for 0% -> 0%
where the time goes in v1:
time: 29.9 us; the launch traced here: 29.6 us
  Pallas kernels  22.4 us (75%)
  local copies, waits for them, and re-layouts  6.62 us (22%)
  between operations  0.65 us (2%)
    pallas_call x1, Pallas kernels, on_device(): pl.pallas_call(functools.partial(kernel, groups, clips, per, patches * gr...  22.4 us
    unnamed x13, local copies, waits for them, and re-layouts  6.62 us

profile of v1, /device:TPU:0, one launch (start us, length us, event | category | flops | bytes accessed | tf_op | source)
XLA Modules:
  0.0 29.6 jit_solution(17791611117142468981)
XLA Ops:
  0.6 0.0 copy-start
  0.6 1.3 %copy-done = bf16[768,768]{1,0:T(8,128)(2,1)S(1)} copy-done((bf16[768,768]{1,0:T(8,128)(2,1)S(1)}, bf16[768,768]{1,0:T(8,128)(2,1)}, u32[]{:S(2)}) %copy-start) | copy-done | bytes 1179672
  1.9 0.0 copy-start.1
  1.9 1.3 %copy-done.1 = bf16[768,768]{1,0:T(8,128)(2,1)S(1)} copy-done((bf16[768,768]{1,0:T(8,128)(2,1)S(1)}, bf16[768,768]{1,0:T(8,128)(2,1)}, u32[]{:S(2)}) %copy-start.1) | copy-done | bytes 1179672
  3.2 0.0 copy-start.2
  3.2 0.9 %copy-done.2 = bf16[1,1,128,768]{3,2,1,0:T(8,128)(2,1)S(1)} copy-done((bf16[1,1,128,768]{3,2,1,0:T(8,128)(2,1)S(1)}, bf16[1,1,128,768]{3,2,1,0:T(8,128)(2,1)}, u32[]{:S(2)}) %copy-start.2) | copy-done | bytes 196632
  4.1 0.0 copy-start.3
  4.1 0.7 %copy-done.3 = f32[4,768]{1,0:T(4,128)S(1)} copy-done((f32[4,768]{1,0:T(4,128)S(1)}, f32[4,768]{1,0:T(4,128)}, u32[]{:S(2)}) %copy-start.3) | copy-done | bytes 12312
  4.8 0.0 copy-start.4
  4.8 0.7 %copy-done.4 = f32[2,768]{1,0:T(2,128)S(1)} copy-done((f32[2,768]{1,0:T(2,128)S(1)}, f32[2,768]{1,0:T(2,128)}, u32[]{:S(2)}) %copy-start.4) | copy-done | bytes 6168
  5.5 22.4 %shard_map.94 = (bf16[128,768]{1,0:T(8,128)(2,1)S(1)}, f32[1,768]{1,0:T(1,128)S(1)}, f32[1,4]{1,0:T(1,128)S(1)}) custom-call(bf16[128,768]{1,0:T(8,128)(2,1)S(1)} %bitcast.3, f32[2,768]{1,0:T(2,128)S(1)} %copy-done.4, bf16[768,2304]{1,0:T(8,128)(2,1)} %space_proj_hbm.1, bf16[768,768]{1,0:T(8,128)(2,1)S(1)} %copy-done, bf16[768,2304]{1,0:T(8,128)(2,1)} %time_proj_hbm.1, ...), custom_call_target="tpu_custom_call" | custom-call | tf_op jit(solution)/shard_map/pallas_call | solution.py:201
  27.9 0.7 %copy.13 = bf16[1,1,128,768]{3,2,1,0:T(8,128)(2,1)} copy(bf16[1,1,128,768]{3,2,1,0:T(8,128)(2,1)S(1)} %bitcast.2) | data formatting | bytes 393216
  28.5 0.6 %copy.14 = f32[1,768]{1,0:T(1,128)} copy(f32[1,768]{1,0:T(1,128)S(1)} %get-tuple-element.13) | data formatting | bytes 6144
  29.1 0.5 %copy.15 = f32[1,4]{1,0:T(1,128)} copy(f32[1,4]{1,0:T(1,128)S(1)} %get-tuple-element.14) | data formatting | bytes 32
Async XLA Ops:
  0.6 1.3 %copy-start = (bf16[768,768]{1,0:T(8,128)(2,1)S(1)}, bf16[768,768]{1,0:T(8,128)(2,1)}, u32[]{:S(2)}) copy-start(bf16[768,768]{1,0:T(8,128)(2,1)} %space_out_hbm.1) | copy-start | bytes 3538948
  1.9 1.3 %copy-start.1 = (bf16[768,768]{1,0:T(8,128)(2,1)S(1)}, bf16[768,768]{1,0:T(8,128)(2,1)}, u32[]{:S(2)}) copy-start(bf16[768,768]{1,0:T(8,128)(2,1)} %time_out_hbm.1) | copy-start | bytes 3538948
  3.2 0.9 %copy-start.2 = (bf16[1,1,128,768]{3,2,1,0:T(8,128)(2,1)S(1)}, bf16[1,1,128,768]{3,2,1,0:T(8,128)(2,1)}, u32[]{:S(2)}) copy-start(bf16[1,1,128,768]{3,2,1,0:T(8,128)(2,1)} %param.7) | copy-start | bytes 589828
  4.1 0.7 %copy-start.3 = (f32[4,768]{1,0:T(4,128)S(1)}, f32[4,768]{1,0:T(4,128)}, u32[]{:S(2)}) copy-start(f32[4,768]{1,0:T(4,128)} %qk_ref.1) | copy-start | bytes 36868
  4.8 0.7 %copy-start.4 = (f32[2,768]{1,0:T(2,128)S(1)}, f32[2,768]{1,0:T(2,128)}, u32[]{:S(2)}) copy-start(f32[2,768]{1,0:T(2,128)} %norm_ref.1) | copy-start | bytes 18436

commit v2 on v1

--- a/solution.py
+++ b/solution.py
@@ -16,12 +16,12 @@
 F32 = jnp.float32
 
 
-def each(count, body):
+def each(count, body, first=1):
     if count <= 8:
-        for at in range(1, count):
+        for at in range(first, count):
             body(at)
     else:
-        lax.fori_loop(1, count, lambda at, carry: (body(at), carry)[1], 0)
+        lax.fori_loop(first, count, lambda at, carry: (body(at), carry)[1], 0)
 
 
 def layer_norm(widened, gain):
@@ -49,9 +49,9 @@
         mean = jnp.dot((values * values).astype(BF16), averager, preferred_element_type=F32)
         return (values * lax.rsqrt(mean + 1e-06) * gain).astype(BF16)
 
-    waits[0]()
     context = []
     for at in range(0, D, WIDE):
+        waits[at // WIDE]()
         queries = normed(at, gains[query_row : query_row + 1, at : at + WIDE] * (HEAD ** -0.5))
         keys = normed(D + at, gains[query_row + 1 : query_row + 2, at : at + WIDE])
         values = part(2 * D + at)
@@ -73,31 +73,42 @@
             )
             both = jnp.dot(raised, value_pair, preferred_element_type=F32)
             context.append((both[:, : 2 * HEAD] / both[:, 2 * HEAD :]).astype(BF16))
-    waits[1]()
+    waits[-1]()
     return jnp.dot(jnp.concatenate(context, axis=1), out_weight[...], preferred_element_type=F32)
 
 
 def kernel(
     groups, clips, per, tokens_in_clip,
-    frames_ref, norm_ref, space_proj_hbm, space_out_hbm, time_proj_hbm, time_out_hbm, qk_ref,
+    frames_hbm, norm_hbm, space_proj_hbm, space_out_hbm, time_proj_hbm, time_out_hbm, qk_hbm,
     block_ref, embed_ref, similar_ref,
-    space_proj, space_out, time_proj, time_out,
+    frames_ref, norm_ref, qk_ref, space_proj, space_out, time_proj, time_out,
     outgoing, arrived, branch_out, returned, sums, embeds,
-    weight_sem, out_send, out_recv, back_send, back_recv, sum_send, sum_recv, embed_send, embed_recv,
+    load_sem, out_send, out_recv, back_send, back_recv, sum_send, sum_recv, embed_send, embed_recv,
 ):
     me = lax.axis_index("seq")
     clip = lax.axis_index("clip")
     patches = frames_ref.shape[0]
     padded = outgoing.shape[1]
 
+    pieces = [(frames_hbm, frames_ref), (norm_hbm, norm_ref), (qk_hbm, qk_ref)]
+    for source, target, out_source, out_target in (
+        (space_proj_hbm, space_proj, space_out_hbm, space_out), (time_proj_hbm, time_proj, time_out_hbm, time_out)):
+        for at in range(0, D, WIDE):
+            for start in (at, D + at, 2 * D + at):
+                columns = pl.ds(start, WIDE)
+                pieces.append((source.at[:, columns], target.at[:, columns]))
+        pieces.append((out_source, out_target))
     loads = [
-        pltpu.make_async_copy(source, target, weight_sem.at[at])
-        for at, (source, target) in enumerate(
-            [(space_proj_hbm, space_proj), (space_out_hbm, space_out), (time_proj_hbm, time_proj), (time_out_hbm, time_out)]
-        )
-    ]
+        pltpu.make_async_copy(source, target, load_sem.at[at]) for at, (source, target) in enumerate(pieces)]
     for load in loads:
         load.start()
+
+    def waits(first):
+        def wait(some):
+            for load in some:
+                load.wait()
+        parts = [loads[first + 3 * at : first + 3 * at + 3] for at in range(D // WIDE)]
+        return [functools.partial(wait, part) for part in parts + [loads[first + 9 : first + 10]]]
 
     barrier = pltpu.get_barrier_semaphore()
     each(groups, lambda d: pl.semaphore_signal(
@@ -126,10 +137,12 @@
             src_ref=embeds.at[clip], dst_ref=embeds.at[clip], send_sem=embed_send.at[d], recv_sem=embed_recv.at[d],
             device_id={"clip": lax.rem(clip + d, clips)}, device_id_type=MESH)
 
+    for load in loads[:3]:
+        load.wait()
     frames = frames_ref[...].astype(F32)
     spread_out = attend(
         layer_norm(frames, norm_ref[0:1, :]), space_proj, space_out, qk_ref, 0, None,
-        (loads[0].wait, loads[1].wait))
+        waits(3))
     middle = (frames + spread_out).astype(BF16)
     widened = middle.astype(F32)
     ready = layer_norm(widened, norm_ref[1:2, :])
@@ -155,13 +168,13 @@
         tokens = jnp.dot(gather, tokens, preferred_element_type=F32).astype(BF16)
     branch = attend(
         tokens, time_proj, time_out, qk_ref, 2, jnp.concatenate([same, same], axis=1),
-        (loads[2].wait, loads[3].wait)).astype(BF16)
+        waits(13)).astype(BF16)
     sums[0] = own_sum + jnp.sum(branch.astype(F32), axis=0, keepdims=True)
     each(groups, lambda d: share(d).start())
     if padded != per:
         branch = jnp.dot(spread, branch, preferred_element_type=F32).astype(BF16)
     branch_out[...] = branch.reshape(branch_out.shape)
-    each(groups, lambda d: homeward(d).start())
+    each(groups // 2, lambda d: homeward(d).start())
     returned[me] = branch_out[0]
 
     each(groups, lambda d: share(d).wait_recv())
@@ -169,6 +182,7 @@
     embed = pooled * lax.rsqrt(jnp.mean(pooled * pooled, axis=-1, keepdims=True) + 1e-06)
     embeds[clip] = embed
     each(clips, lambda d: announce(d).start())
+    each(groups, lambda d: homeward(d).start(), groups // 2)
     embed_ref[...] = embed
 
     each(groups, lambda d: homeward(d).wait_recv())
@@ -187,6 +201,18 @@
     each(groups, lambda d: share(d).wait_send())
     each(groups, lambda d: homeward(d).wait_send())
     each(clips, lambda d: announce(d).wait_send())
+
+
+def write_out(block_ref, embed_ref, similar_ref, block_hbm, embed_hbm, similar_hbm, store_sem):
+    stores = [
+        pltpu.make_async_copy(source, target, store_sem.at[at])
+        for at, (source, target) in enumerate(
+            [(block_ref, block_hbm), (embed_ref, embed_hbm), (similar_ref, similar_hbm)])
+    ]
+    for store in stores:
+        store.start()
+    for store in stores:
+        store.wait()
 
 
 def on_device(frames_in, norm_gains, space_proj, space_out, time_proj, time_out, qk_gains):
@@ -195,19 +221,19 @@
     per = patches // groups
     padded = -(-per // 16) * 16
     vmem = pl.BlockSpec(memory_space=pltpu.VMEM)
-    hbm = pl.BlockSpec(memory_space=pl.ANY)
+    hbm = pl.BlockSpec(memory_space=pltpu.HBM)
     blocks = pltpu.VMEM((groups, padded, channels), BF16)
     dma = pltpu.SemaphoreType.DMA
     block, embed, similar = pl.pallas_call(
         functools.partial(kernel, groups, clips, per, patches * groups),
         out_shape=(
-            jax.ShapeDtypeStruct((patches, channels), BF16),
-            jax.ShapeDtypeStruct((1, channels), F32),
-            jax.ShapeDtypeStruct((1, clips), F32),
-        ),
-        in_specs=[vmem, vmem, hbm, hbm, hbm, hbm, vmem],
+            pltpu.VMEM((patches, channels), BF16), pltpu.VMEM((1, channels), F32), pltpu.VMEM((1, clips), F32)),
+        in_specs=[hbm] * 7,
         out_specs=(vmem, vmem, vmem),
         scratch_shapes=[
+            pltpu.VMEM((patches, channels), BF16),
+            pltpu.VMEM(norm_gains.shape, F32),
+            pltpu.VMEM(qk_gains.shape, F32),
             pltpu.VMEM(space_proj.shape, BF16),
             pltpu.VMEM(space_out.shape, BF16),
             pltpu.VMEM(time_proj.shape, BF16),
@@ -215,13 +241,25 @@
             blocks, blocks, blocks, blocks,
             pltpu.VMEM((groups, 1, channels), F32),
             pltpu.VMEM((clips, 1, channels), F32),
-            dma((4,)),
+            dma((23,)),
             dma((groups,)), dma((groups,)), dma((groups,)), dma((groups,)),
             dma((groups,)), dma((groups,)), dma((clips,)), dma((clips,)),
         ],
         compiler_params=pltpu.CompilerParams(
-            collective_id=0, has_side_effects=True, vmem_limit_bytes=48 * 1024 * 1024),
+            collective_id=0, has_side_effects=True, vmem_limit_bytes=62 * 1024 * 1024),
     )(frames_in.reshape(patches, channels), norm_gains, space_proj, space_out, time_proj, time_out, qk_gains)
+    block, embed, similar = pl.pallas_call(
+        write_out,
+        out_shape=(
+            jax.ShapeDtypeStruct((patches, channels), BF16),
+            jax.ShapeDtypeStruct((1, channels), F32),
+            jax.ShapeDtypeStruct((1, clips), F32),
+        ),
+        in_specs=[vmem] * 3,
+        out_specs=(hbm, hbm, hbm),
+        scratch_shapes=[dma((3,))],
+        compiler_params=pltpu.CompilerParams(vmem_limit_bytes=1024 * 1024),
+    )(block, embed, similar)
     return block.reshape(frames_in.shape), embed, similar
 
 

time: 29.9 us -> 24.6 us (0.82)
  local copies, waits for them, and re-layouts: 6.62 us -> 0 us
  Pallas kernels: 22.4 us -> 23.8 us
    unnamed x13 -> x0, local copies, waits for them, and re-layouts: 6.62 us -> none
    pallas_call x1, Pallas kernels: 22.4 us -> 23.1 us  [on_device(): pl.pallas_call(functools.partial(kernel, groups, clips, per, patches * gr...]
    pallas_call x0 -> x1, Pallas kernels: none -> 0.71 us  [on_device(): pl.pallas_call(write_out, out_shape=(jax.ShapeDtypeStruct((patches, chann...]
where the time goes in v2:
time: 24.6 us; the launch traced here: 24.4 us
  Pallas kernels  23.8 us (97%)
  between operations  0.64 us (3%)
    pallas_call x1, Pallas kernels, on_device(): pl.pallas_call(functools.partial(kernel, groups, clips, per, patches * gr...  23.1 us
    pallas_call x1, Pallas kernels, on_device(): pl.pallas_call(write_out, out_shape=(jax.ShapeDtypeStruct((patches, chann...  0.71 us

profile of v2, /device:TPU:0, one launch (start us, length us, event | category | flops | bytes accessed | tf_op | source)
XLA Modules:
  0.0 24.4 jit_solution(6070957890353891088)
XLA Ops:
  0.6 23.1 %shard_map.94 = (bf16[128,768]{1,0:T(8,128)(2,1)S(1)}, f32[1,768]{1,0:T(1,128)S(1)}, f32[1,4]{1,0:T(1,128)S(1)}) custom-call(bf16[128,768]{1,0:T(8,128)(2,1)} %bitcast.2, f32[2,768]{1,0:T(2,128)} %norm_hbm.1, bf16[768,2304]{1,0:T(8,128)(2,1)} %space_proj_hbm.1, bf16[768,768]{1,0:T(8,128)(2,1)} %space_out_hbm.1, bf16[768,2304]{1,0:T(8,128)(2,1)} %time_proj_hbm.1, ...), custom_call_target="tpu_custom_call" | custom-call | tf_op jit(solution)/shard_map/pallas_call | solution.py:227
  23.7 0.7 %shard_map.95 = (bf16[128,768]{1,0:T(8,128)(2,1)}, f32[1,768]{1,0:T(1,128)}, f32[1,4]{1,0:T(1,128)}) custom-call(bf16[128,768]{1,0:T(8,128)(2,1)S(1)} %get-tuple-element.9.block_ref, f32[1,768]{1,0:T(1,128)S(1)} %get-tuple-element.10.embed_ref, f32[1,4]{1,0:T(1,128)S(1)} %get-tuple-element.11.similar_ref), custom_call_target="tpu_custom_call" | custom-call | tf_op jit(solution)/shard_map/pallas_call | solution.py:251
